TPU v7x, 32 devices: a whole 2x2x4 slice. The times are simulated.
32 devices in a mesh: dp: 4 (over z), ctx: 8 (over y, x, core).
Axes of the slice: x: 2, y: 2, z: 4, core: 2. Of those that a mesh axis runs over, the one named last changes fastest.
Arguments:
- queries: bfloat16 [4, 1024, 4096], P('dp', 'ctx'), may hold values from -216 to 216
- keys: bfloat16 [4, 1024, 1024], P('dp', 'ctx'), may hold values from -6 to 6
- values: bfloat16 [4, 1024, 1024], P('dp', 'ctx'), may hold values from -6 to 6
- out_grad: bfloat16 [4, 1024, 4096], P('dp', 'ctx'), may hold values from -6 to 6
- block_mask: int32 [32, 8, 8], replicated, may hold values from 0 to 1, as said below
Outputs:
- query_grad: bfloat16 [4, 1024, 4096], P('dp', 'ctx')
- key_grad: bfloat16 [4, 1024, 1024], P('dp', 'ctx')
- value_grad: bfloat16 [4, 1024, 1024], P('dp', 'ctx')
- z_loss: float32 [32], P('ctx')
Inputs may be any that keep to these rules, and one draw needn't show every extreme that they name: block_mask[h, a, b] is 1 only where b <= a; block_mask[h, a, a] = 1 and block_mask[h, a, 0] = 1 for every head h and query block a.
All inputs are finite; a program needn't handle non-finite values.
Results may differ from a plain program's by a relative error of at most 0.014.
Values may be sent and summed in bfloat16 or wider, within the bound.
A program may use at most 128 MiB of HBM per device.

v0:
```python
import functools
import math

import jax
import jax.numpy as jnp
from jax import lax
from jax.experimental import pallas as pl
from jax.experimental.pallas import tpu as pltpu
from jax.sharding import PartitionSpec as P

H = 32
KVH = 8
HD = 128
BLK = 128
ZLOSS = 0.05
NEG = -1e30
TILE = 2 * BLK
MESH = pl.DeviceIdType.MESH
LOG2E = math.log2(math.e)
LN2 = math.log(2.0)


def dot(a, b):
    return jnp.dot(a, b, preferred_element_type=jnp.float32)


def steps(count, step, state):
    if isinstance(count, int) and count <= 4:
        for i in range(count):
            state = step(i, state)
        return state
    return lax.fori_loop(0, count, step, state)


def rows(i, size):
    return pl.ds(i * size if isinstance(i, int) else pl.multiple_of(i * size, size), size)


def fold(x, op):
    return op(x.reshape(x.shape[0] // 8, 8, x.shape[1]), axis=0)


def kernel(
    sizes,
    mask, q_in, g_in, k_in, v_in,
    dq_out, dk_out, dv_out, z_out,
    q_all, g_all, k_all, v_all, k_tr, v_tr,
    score, dk_acc, dv_acc, dq_buf, dk_buf, dv_buf, z_own, z_all,
    q_sem, g_sem, kv_sem, out_sem, send_sem, z_sem,
):
    n, dp, per, share, tok = sizes
    seq = n * tok
    tiles = seq // TILE
    me = lax.axis_index("ctx")
    my_dp = lax.axis_index("dp")
    group = H // KVH
    scale = HD ** (-0.5)

    barrier = pltpu.get_barrier_semaphore()

    def greet(j, c):
        pl.semaphore_signal(
            barrier, inc=1, device_id=(my_dp, lax.rem(me + j, n)), device_id_type=MESH
        )
        return c

    def greet_dp(j, c):
        pl.semaphore_signal(
            barrier, inc=1, device_id=(lax.rem(my_dp + j, dp), me), device_id_type=MESH
        )
        return c

    lax.fori_loop(1, n, greet, 0)
    lax.fori_loop(1, dp, greet_dp, 0)
    pl.semaphore_wait(barrier, n - 1 + dp - 1)

    def lanes(i):
        return pl.ds(pl.multiple_of(i * HD, HD), HD)

    def remote(src, dst, send, recv, target):
        pltpu.make_async_remote_copy(
            src_ref=src, dst_ref=dst, send_sem=send, recv_sem=recv,
            device_id=(my_dp, target), device_id_type=MESH,
        ).start()

    mine = rows(me, tok)

    def kv_head(device):
        return (device * per) // group

    def send_kv(j, c):
        to = lax.rem(me + j, n)
        col = lanes(kv_head(to))
        remote(k_in.at[0, :, col], k_all.at[mine], send_sem.at[0], kv_sem.at[0], to)
        remote(v_in.at[0, :, col], v_all.at[mine], send_sem.at[1], kv_sem.at[1], to)
        return c

    lax.fori_loop(1, n, send_kv, 0)
    own = lanes(kv_head(me))
    pltpu.make_async_copy(k_in.at[0, :, own], k_all.at[mine], kv_sem.at[0]).start()
    pltpu.make_async_copy(v_in.at[0, :, own], v_all.at[mine], kv_sem.at[1]).start()

    def send_head(h, c):
        def send_q(j, c):
            to = lax.rem(me + j, n)
            col = lanes(to * per + h)
            remote(q_in.at[0, :, col], q_all.at[h, mine], send_sem.at[2], q_sem.at[h], to)
            remote(g_in.at[0, :, col], g_all.at[h, mine], send_sem.at[3], g_sem.at[h], to)
            return c

        lax.fori_loop(1, n, send_q, 0)
        col = lanes(me * per + h)
        pltpu.make_async_copy(q_in.at[0, :, col], q_all.at[h, mine], q_sem.at[h]).start()
        pltpu.make_async_copy(g_in.at[0, :, col], g_all.at[h, mine], g_sem.at[h]).start()
        return c

    lax.fori_loop(0, per, send_head, 0)

    def wait_for(ref, sem):
        pltpu.make_async_copy(ref, ref, sem).wait()

    z_own[...] = jnp.zeros_like(z_own)
    dk_acc[...] = jnp.zeros_like(dk_acc)
    dv_acc[...] = jnp.zeros_like(dv_acc)
    wait_for(k_all, kv_sem.at[0])
    wait_for(v_all, kv_sem.at[1])

    def turn(c, s):
        at = rows(c, TILE)
        k_tr[:, at] = k_all[at].astype(jnp.float32).T.astype(jnp.bfloat16)
        v_tr[:, at] = v_all[at].astype(jnp.float32).T.astype(jnp.bfloat16)
        return s

    steps(tiles, turn, 0)
    first_half = lax.broadcasted_iota(jnp.int32, (1, TILE), 1) < BLK
    causal = lax.broadcasted_iota(jnp.int32, (TILE, TILE), 0) <= lax.broadcasted_iota(
        jnp.int32, (TILE, TILE), 1
    )

    def one_head(h, c):
        wait_for(q_all.at[h], q_sem.at[h])
        wait_for(g_all.at[h], g_sem.at[h])
        head = me * per + h

        def one_tile(t):
            q_at = rows(t, TILE)
            q = q_all[h, q_at, :]
            g = g_all[h, q_at, :]
            q_tr = q.astype(jnp.float32).T.astype(jnp.bfloat16)
            g_f32 = g.astype(jnp.float32).T
            g_tr = g_f32.astype(jnp.bfloat16)

            def bias(c):
                parts = []
                for b in range(2):
                    left = mask[2 * t, 2 * c + b, head]
                    right = mask[2 * t + 1, 2 * c + b, head]
                    on = jnp.where(first_half, left, right).astype(jnp.float32)
                    parts.append(jnp.broadcast_to((1.0 - on) * NEG, (BLK, TILE)))
                return jnp.concatenate(parts, axis=0)

            def score_chunk(c, top, diagonal):
                at = rows(c, TILE)
                s = dot(k_all[at], q_tr) * (scale * LOG2E) + bias(c)
                if diagonal:
                    s = jnp.where(causal, s, NEG)
                score[at] = s
                return jnp.maximum(top, fold(s, jnp.max))

            top = jnp.full((8, TILE), NEG, jnp.float32)
            top = steps(t, lambda c, x: score_chunk(c, x, False), top)
            top = score_chunk(t, top, True)
            top = jnp.max(top, axis=0, keepdims=True)

            def exp_chunk(c, state):
                total, out = state
                at = rows(c, TILE)
                e = jnp.exp2(score[at] - top)
                score[at] = e
                out = out + dot(v_tr[:, at], e.astype(jnp.bfloat16))
                return total + fold(e, jnp.sum), out

            total, out = steps(
                t + 1, exp_chunk,
                (jnp.zeros((8, TILE), jnp.float32), jnp.zeros((HD, TILE), jnp.float32)),
            )
            total = jnp.sum(total, axis=0, keepdims=True)
            inverse = 1.0 / total
            out = (out * inverse).astype(jnp.bfloat16).astype(jnp.float32)
            delta = jnp.sum(g_f32 * out, axis=0, keepdims=True)
            log_norm = top * LN2 + jnp.log(total)
            shift = delta - (2.0 * ZLOSS) * log_norm
            square = log_norm * log_norm
            z_own[pl.ds(h, 1), :] += square[:, :BLK] + square[:, BLK:]

            def grad_chunk(c, dq):
                at = rows(c, TILE)
                p = score[at] * inverse
                dv_acc[at] += dot(p.astype(jnp.bfloat16), g)
                ds = (p * (dot(v_all[at], g_tr) - shift)).astype(jnp.bfloat16)
                dk_acc[at] += dot(ds, q)
                return dq + dot(k_tr[:, at], ds)

            dq = steps(t + 1, grad_chunk, jnp.zeros((HD, TILE), jnp.float32))
            dq_buf[h, q_at, :] = (dq * scale).T.astype(jnp.bfloat16)

            for part in range(TILE // tok):
                to = t * (TILE // tok) + part
                src = dq_buf.at[h, rows(to, tok)]
                dst = dq_out.at[0, :, lanes(head)]

                @pl.when(me == to)
                def _():
                    pltpu.make_async_copy(src, dst, out_sem.at[0]).start()

                @pl.when(me != to)
                def _():
                    remote(src, dst, send_sem.at[4], out_sem.at[0], to)

            @pl.when(h == per - 1)
            def _():
                dk_buf[q_at] = (dk_acc[q_at] * scale).astype(jnp.bfloat16)
                dv_buf[q_at] = dv_acc[q_at].astype(jnp.bfloat16)
                slot = lax.rem(me, share)
                col = lanes(kv_head(me))
                for part in range(TILE // tok):
                    to = t * (TILE // tok) + part
                    src_k = dk_buf.at[rows(to, tok)]
                    src_v = dv_buf.at[rows(to, tok)]

                    @pl.when(me == to)
                    def _():
                        pltpu.make_async_copy(src_k, dk_out.at[slot, :, col], out_sem.at[1]).start()
                        pltpu.make_async_copy(src_v, dv_out.at[slot, :, col], out_sem.at[2]).start()

                    @pl.when(me != to)
                    def _():
                        remote(src_k, dk_out.at[slot, :, col], send_sem.at[5], out_sem.at[1], to)
                        remote(src_v, dv_out.at[slot, :, col], send_sem.at[6], out_sem.at[2], to)

        if tiles <= 4:
            for t in reversed(range(tiles)):
                one_tile(t)
        else:
            def tile_step(i, s):
                one_tile(tiles - 1 - i)
                return s

            lax.fori_loop(0, tiles, tile_step, 0)
        return c

    lax.fori_loop(0, per, one_head, 0)

    pltpu.make_async_copy(z_own, z_all.at[my_dp], z_sem.at[1]).start()

    def send_z(j, c):
        pltpu.make_async_remote_copy(
            src_ref=z_own, dst_ref=z_all.at[my_dp], send_sem=z_sem.at[0], recv_sem=z_sem.at[1],
            device_id=(lax.rem(my_dp + j, dp), me), device_id_type=MESH,
        ).start()
        return c

    lax.fori_loop(1, dp, send_z, 0)
    wait_for(z_all, z_sem.at[1])
    z_sum = jnp.sum(jnp.sum(z_all[...], axis=0), axis=1, keepdims=True)
    z_out[...] = jnp.broadcast_to(z_sum * (ZLOSS / (seq * dp)), z_out.shape)

    wait_for(dq_out, out_sem.at[0])
    wait_for(dk_out, out_sem.at[1])
    wait_for(dv_out, out_sem.at[2])
    others = pl.ds(0, seq - tok)
    wide = pl.ds(0, (n - 1) * per * HD)
    wait_for(k_all.at[others], send_sem.at[0])
    wait_for(v_all.at[others], send_sem.at[1])
    wait_for(q_in.at[0, :, wide], send_sem.at[2])
    wait_for(g_in.at[0, :, wide], send_sem.at[3])
    wait_for(dq_out.at[0, :, wide], send_sem.at[4])
    wait_for(dk_buf.at[others], send_sem.at[5])
    wait_for(dv_buf.at[others], send_sem.at[6])
    wait_for(z_all.at[pl.ds(0, dp - 1)], z_sem.at[0])


def body(queries, keys, values, out_grad, block_mask):
    tok = queries.shape[1]
    n = lax.axis_size("ctx")
    dp = lax.axis_size("dp")
    per = H // n
    share = max(1, n // KVH)
    seq = tok * n
    low, wide = jnp.bfloat16, jnp.float32
    anywhere = pl.BlockSpec(memory_space=pl.ANY)
    dq, dk, dv, z = pl.pallas_call(
        functools.partial(kernel, (n, dp, per, share, tok)),
        out_shape=(
            jax.ShapeDtypeStruct(queries.shape, low),
            jax.ShapeDtypeStruct((share, tok, KVH * HD), low),
            jax.ShapeDtypeStruct((share, tok, KVH * HD), low),
            jax.ShapeDtypeStruct((8, BLK), wide),
        ),
        in_specs=[pl.BlockSpec(memory_space=pltpu.SMEM)] + [anywhere] * 4,
        out_specs=(anywhere, anywhere, anywhere, pl.BlockSpec(memory_space=pltpu.VMEM)),
        scratch_shapes=[
            pltpu.VMEM((per, seq, HD), low),
            pltpu.VMEM((per, seq, HD), low),
            pltpu.VMEM((seq, HD), low),
            pltpu.VMEM((seq, HD), low),
            pltpu.VMEM((HD, seq), low),
            pltpu.VMEM((HD, seq), low),
            pltpu.VMEM((seq, TILE), wide),
            pltpu.VMEM((seq, HD), wide),
            pltpu.VMEM((seq, HD), wide),
            pltpu.VMEM((per, seq, HD), low),
            pltpu.VMEM((seq, HD), low),
            pltpu.VMEM((seq, HD), low),
            pltpu.VMEM((8, BLK), wide),
            pltpu.VMEM((dp, 8, BLK), wide),
            pltpu.SemaphoreType.DMA((per,)),
            pltpu.SemaphoreType.DMA((per,)),
            pltpu.SemaphoreType.DMA((2,)),
            pltpu.SemaphoreType.DMA((3,)),
            pltpu.SemaphoreType.DMA((7,)),
            pltpu.SemaphoreType.DMA((2,)),
        ],
        compiler_params=pltpu.CompilerParams(
            collective_id=0, has_side_effects=True, vmem_limit_bytes=62 * 1024 * 1024
        ),
        name="attention_exchange",
    )(block_mask.transpose(1, 2, 0), queries, out_grad, keys, values)
    if share > 1:
        dk = jnp.sum(dk.astype(wide), axis=0, keepdims=True).astype(low)
        dv = jnp.sum(dv.astype(wide), axis=0, keepdims=True).astype(low)
    return (dq, dk, dv, z[:per, 0])


def quad_kernel(
    dp,
    mask, q_in, g_in, k_in, v_in,
    dq_out, dk_out, dv_out, z_out,
    q_all, g_all, k_all, v_all, k_tr, v_tr,
    score, p_low, ds_low, dk_acc, dv_acc, dq_buf, dk_buf, dv_buf, dk_part, dv_part, z_own, z_set, z_all,
    q_sem, g_sem, k_sem, v_sem, dq_sem, dk_sem, dv_sem, send_sem, z_sem,
):
    n, tok, per = 8, BLK, H // KVH
    seq = n * tok
    me = lax.axis_index("ctx")
    my_dp = lax.axis_index("dp")
    y, x, core = me // 4, lax.rem(me // 2, 2), lax.rem(me, 2)
    chip = me // 2
    scale = HD ** (-0.5)

    barrier = pltpu.get_barrier_semaphore()

    def greet(j, c):
        pl.semaphore_signal(
            barrier, inc=1, device_id=(my_dp, lax.rem(me + j, n)), device_id_type=MESH
        )
        return c

    def greet_dp(j, c):
        pl.semaphore_signal(
            barrier, inc=1, device_id=(lax.rem(my_dp + j, dp), me), device_id_type=MESH
        )
        return c

    lax.fori_loop(1, n, greet, 0)
    lax.fori_loop(1, dp, greet_dp, 0)
    pl.semaphore_wait(barrier, n - 1 + dp - 1)

    def lanes(i):
        return pl.ds(pl.multiple_of(i * HD, HD), HD)

    def remote(src, dst, send, recv, target):
        pltpu.make_async_remote_copy(
            src_ref=src, dst_ref=dst, send_sem=send, recv_sem=recv,
            device_id=(my_dp, target), device_id_type=MESH,
        ).start()

    def move(src, dst, send, recv, target):
        @pl.when(target == me)
        def _():
            pltpu.make_async_copy(src, dst, recv).start()

        @pl.when(target != me)
        def _():
            remote(src, dst, send, recv, target)

    def wait_for(ref, sem):
        pltpu.make_async_copy(ref, ref, sem).wait()

    def kv_head(group, to):
        first = 2 * lax.rem(to // 2, 2) + lax.rem(to, 2)
        second = 4 + 2 * (to // 4) + lax.rem(to, 2)
        return first if group == 0 else second

    mine = rows(me, tok)

    def send_kv(group):
        def one(j, c):
            to = lax.rem(me + j, n)
            last = 2 * (to // 4) + 1 if group == 0 else 2 + lax.rem(to // 2, 2)

            @pl.when(chip <= last)
            def _():
                col = lanes(kv_head(group, to))
                move(k_in.at[0, :, col], k_all.at[group, mine], send_sem.at[group],
                     k_sem.at[group * 4 + chip], to)
                move(v_in.at[0, :, col], v_all.at[group, mine], send_sem.at[2 + group],
                     v_sem.at[group * 4 + chip], to)

            return c

        lax.fori_loop(0, n, one, 0)

    def send_q(group, m):
        item = 2 * m + group
        slot = x if group == 0 else y
        place = rows(2 * slot + core, tok)

        def one(j, c):
            far = lax.rem((x if group == 0 else y) + j // 2, 2)
            to = 2 * far + lax.rem(core + j, 2) + (4 * y if group == 0 else 0)
            if group == 1:
                to = 4 * far + 2 * x + lax.rem(core + j, 2)
            col = lanes(kv_head(group, to) * per + m)
            at = item * 2 + slot
            move(q_in.at[0, :, col], q_all.at[item, place], send_sem.at[4], q_sem.at[at], to)
            move(g_in.at[0, :, col], g_all.at[item, place], send_sem.at[5], g_sem.at[at], to)
            return c

        lax.fori_loop(0, 4, one, 0)

    def send_pair(m, c):
        send_q(0, m)
        send_q(1, m)
        return c

    send_kv(0)
    send_q(0, 0)
    send_kv(1)
    send_q(1, 0)
    lax.fori_loop(1, per, send_pair, 0)

    z_own[...] = jnp.zeros_like(z_own)
    dk_acc[...] = jnp.zeros_like(dk_acc)
    dv_acc[...] = jnp.zeros_like(dv_acc)
    first_half = lax.broadcasted_iota(jnp.int32, (1, TILE), 1) < BLK
    causal = lax.broadcasted_iota(jnp.int32, (TILE, TILE), 0) <= lax.broadcasted_iota(
        jnp.int32, (TILE, TILE), 1
    )

    def prepare(group, last):
        def one(c, carry):
            at = rows(c, TILE)
            wait_for(k_all.at[group, at], k_sem.at[group * 4 + c])
            wait_for(v_all.at[group, at], v_sem.at[group * 4 + c])
            k_tr[group, :, at] = k_all[group, at, :].astype(jnp.float32).T.astype(jnp.bfloat16)
            v_tr[group, :, at] = v_all[group, at, :].astype(jnp.float32).T.astype(jnp.bfloat16)
            return carry

        lax.fori_loop(0, last + 1, one, 0)

    def tile_pair(pair, group, head, item):
        work = []
        for slot, t in ((1, pair[1]), (0, pair[0])):
            q = q_all[item, rows(slot, TILE), :]
            g = g_all[item, rows(slot, TILE), :]
            g_f32 = g.astype(jnp.float32).T
            work.append(dict(
                slot=slot, t=t, span=pl.ds(0, (t + 1) * TILE), q=q, g=g, g_f32=g_f32,
                q_tr=q.astype(jnp.float32).T.astype(jnp.bfloat16), g_tr=g_f32.astype(jnp.bfloat16),
            ))

        def bias(t, c):
            parts = []
            for b in range(2):
                left = mask[2 * t, 2 * c + b, head]
                right = mask[2 * t + 1, 2 * c + b, head]
                on = jnp.where(first_half, left, right).astype(jnp.float32)
                parts.append(jnp.broadcast_to((1.0 - on) * NEG, (BLK, TILE)))
            return jnp.concatenate(parts, axis=0)

        for w in work:
            w["raw"] = dot(k_all[group, w["span"], :], w["q_tr"])
        for w in work:
            t, slot = w["t"], w["slot"]
            top = jnp.full((8, TILE), NEG, jnp.float32)
            for c in range(t + 1):
                s = w["raw"][c * TILE:(c + 1) * TILE] * (scale * LOG2E) + bias(t, c)
                if c == t:
                    s = jnp.where(causal, s, NEG)
                score[slot, rows(c, TILE), :] = s
                top = jnp.maximum(top, fold(s, jnp.max))
            w["top"] = jnp.max(top, axis=0, keepdims=True)
        for w in work:
            w["pull"] = dot(v_all[group, w["span"], :], w["g_tr"])
        for w in work:
            t, slot = w["t"], w["slot"]
            total = jnp.zeros((8, TILE), jnp.float32)
            for c in range(t + 1):
                at = rows(c, TILE)
                e = jnp.exp2(score[slot, at, :] - w["top"])
                score[slot, at, :] = e
                p_low[slot, at, :] = e.astype(jnp.bfloat16)
                total = total + fold(e, jnp.sum)
            w["total"] = jnp.sum(total, axis=0, keepdims=True)
            w["out"] = dot(v_tr[group, :, w["span"]], p_low[slot, w["span"], :])
        square = jnp.zeros((1, TILE), jnp.float32)
        for w in work:
            t, slot = w["t"], w["slot"]
            inverse = 1.0 / w["total"]
            out = (w["out"] * inverse).astype(jnp.bfloat16).astype(jnp.float32)
            delta = jnp.sum(w["g_f32"] * out, axis=0, keepdims=True)
            log_norm = w["top"] * LN2 + jnp.log(w["total"])
            shift = delta - (2.0 * ZLOSS) * log_norm
            square = square + log_norm * log_norm
            for c in range(t + 1):
                at = rows(c, TILE)
                p = score[slot, at, :] * inverse
                ds = p * (w["pull"][c * TILE:(c + 1) * TILE] - shift)
                p_low[slot, at, :] = p.astype(jnp.bfloat16)
                ds_low[slot, at, :] = ds.astype(jnp.bfloat16)
        for w in work:
            slot, span = w["slot"], w["span"]
            dv_acc[group, span, :] += dot(p_low[slot, span, :], w["g"])
            dk_acc[group, span, :] += dot(ds_low[slot, span, :], w["q"])
            dq = dot(k_tr[group, :, span], ds_low[slot, span, :])
            dq_buf[item, rows(slot, TILE), :] = (dq * scale).T.astype(jnp.bfloat16)
        z_own[group, pl.ds(lax.rem(head, per), 1), :] += square[:, :BLK] + square[:, BLK:]

    def one_item(group, m):
        item = 2 * m + group
        half = y if group == 0 else x
        head_kv = kv_head(group, me)
        head = head_kv * per + m
        low = 2 * y if group == 0 else x
        high = 2 * y + 1 if group == 0 else 2 + x

        @pl.when(m == 0)
        def _():
            prepare(group, high)

        for slot in range(2):
            wait_for(q_all.at[item, rows(slot, TILE)], q_sem.at[item * 2 + slot])
            wait_for(g_all.at[item, rows(slot, TILE)], g_sem.at[item * 2 + slot])
        for choice, pair in enumerate(((0, 1), (2, 3)) if group == 0 else ((0, 2), (1, 3))):
            @pl.when(half == choice)
            def _(pair=pair):
                tile_pair(pair, group, head, item)

        def give_dq(i, c):
            tile = jnp.where(i < 2, high, low)
            part = lax.rem(i, 2)
            slot = 1 - i // 2
            move(dq_buf.at[item, rows(2 * slot + part, tok)], dq_out.at[0, :, lanes(head)],
                 send_sem.at[6], dq_sem.at[0], 2 * tile + part)
            return c

        lax.fori_loop(0, 4, give_dq, 0)

        @pl.when(m == per - 1)
        def _():
            sem = group * 2 + half
            col = lanes(head_kv)

            def give(c, carry):
                keys_at = rows(c, TILE)
                dk_buf[group, keys_at, :] = (dk_acc[group, keys_at, :] * scale).astype(jnp.bfloat16)
                dv_buf[group, keys_at, :] = dv_acc[group, keys_at, :].astype(jnp.bfloat16)
                for part in range(2):
                    to = 2 * c + part
                    move(dk_buf.at[group, rows(to, tok)], dk_part.at[half, :, col],
                         send_sem.at[7 + group], dk_sem.at[sem], to)
                    move(dv_buf.at[group, rows(to, tok)], dv_part.at[half, :, col],
                         send_sem.at[9 + group], dv_sem.at[sem], to)
                return carry

            lax.fori_loop(0, high + 1, give, 0)

    def one_step(m, carry):
        one_item(0, m)
        one_item(1, m)
        return carry

    lax.fori_loop(0, per, one_step, 0)

    move(z_own.at[0], z_set.at[y], z_sem.at[0], z_sem.at[2 + y], kv_head(0, me))
    move(z_own.at[1], z_set.at[x], z_sem.at[1], z_sem.at[2 + x], kv_head(1, me))
    wait_for(z_set.at[0], z_sem.at[2])
    wait_for(z_set.at[1], z_sem.at[3])
    z_all[my_dp] = z_set[0] + z_set[1]

    def send_z(j, c):
        pltpu.make_async_remote_copy(
            src_ref=z_all.at[my_dp], dst_ref=z_all.at[my_dp],
            send_sem=z_sem.at[4], recv_sem=z_sem.at[5],
            device_id=(lax.rem(my_dp + j, dp), me), device_id_type=MESH,
        ).start()
        return c

    lax.fori_loop(1, dp, send_z, 0)
    wait_for(z_all.at[pl.ds(0, dp - 1)], z_sem.at[5])
    z_sum = jnp.sum(jnp.sum(z_all[...], axis=0), axis=1, keepdims=True)
    z_out[...] = jnp.broadcast_to(z_sum * (ZLOSS / (seq * dp)), z_out.shape)

    for group in range(2):
        cols = pl.ds(group * 4 * HD, 4 * HD)
        both = (y == 0) if group == 0 else (chip < 3)
        for part, sems, result in ((dk_part, dk_sem, dk_out), (dv_part, dv_sem, dv_out)):
            wait_for(part.at[1, :, cols], sems.at[group * 2 + 1])

            @pl.when(both)
            def _(part=part, sems=sems, result=result):
                wait_for(part.at[0, :, cols], sems.at[group * 2])
                result[0, :, cols] = (
                    part[0, :, cols].astype(jnp.float32) + part[1, :, cols].astype(jnp.float32)
                ).astype(jnp.bfloat16)

            @pl.when(jnp.logical_not(both))
            def _(part=part, result=result):
                result[0, :, cols] = part[1, :, cols]

    wait_for(dq_out, dq_sem.at[0])

    def sent(ref, sem, count):
        wait_for(ref.at[pl.ds(0, count * tok)], sem)

    for group in range(2):
        late = (y == 1) if group == 0 else (chip == 3)
        for sem in (group, 2 + group):
            @pl.when(late)
            def _(sem=sem):
                sent(k_all.at[0], send_sem.at[sem], 3)

            @pl.when(jnp.logical_not(late))
            def _(sem=sem):
                sent(k_all.at[0], send_sem.at[sem], 7)

        whole = (y == 1) if group == 0 else (x == 1)
        for sem in (7 + group, 9 + group):
            @pl.when(whole)
            def _(sem=sem):
                sent(k_all.at[0], send_sem.at[sem], 7)

            @pl.when(jnp.logical_not(whole))
            def _(sem=sem):
                sent(k_all.at[0], send_sem.at[sem], 3 if group == 0 else 5)

        @pl.when(kv_head(group, me) != me)
        def _():
            wait_for(z_own.at[group], z_sem.at[group])

    wide = pl.ds(0, 24 * HD)
    for sem in (4, 5, 6):
        wait_for(dq_out.at[0, :, wide], send_sem.at[sem])
    wait_for(z_all.at[pl.ds(0, dp - 1)], z_sem.at[4])


def finish_kernel(dq, dk, dv, z, dq_out, dk_out, dv_out, z_out, sem):
    copies = [
        pltpu.make_async_copy(a, b, sem.at[i])
        for i, (a, b) in enumerate(((dq, dq_out), (dk, dk_out), (dv, dv_out)))
    ]
    for copy in copies:
        copy.start()
    for h in range(z_out.shape[0]):
        z_out[h] = z[h, 0]
    for copy in copies:
        copy.wait()


def quad_body(queries, keys, values, out_grad, block_mask):
    dp = lax.axis_size("dp")
    seq, items = 8 * BLK, 8
    low, wide = jnp.bfloat16, jnp.float32
    hbm = pl.BlockSpec(memory_space=pltpu.HBM)
    vmem = pl.BlockSpec(memory_space=pltpu.VMEM)
    smem = pl.BlockSpec(memory_space=pltpu.SMEM)
    shape = jax.ShapeDtypeStruct
    results = pl.pallas_call(
        functools.partial(quad_kernel, dp),
        out_shape=(
            shape(queries.shape, low), shape(keys.shape, low), shape(keys.shape, low),
            shape((8, BLK), wide),
        ),
        in_specs=[smem] + [hbm] * 4,
        out_specs=(hbm, vmem, vmem, vmem),
        scratch_shapes=[
            pltpu.VMEM((items, 2 * TILE, HD), low),
            pltpu.VMEM((items, 2 * TILE, HD), low),
            pltpu.VMEM((2, seq, HD), low),
            pltpu.VMEM((2, seq, HD), low),
            pltpu.VMEM((2, HD, seq), low),
            pltpu.VMEM((2, HD, seq), low),
            pltpu.VMEM((2, seq, TILE), wide),
            pltpu.VMEM((2, seq, TILE), low),
            pltpu.VMEM((2, seq, TILE), low),
            pltpu.VMEM((2, seq, HD), wide),
            pltpu.VMEM((2, seq, HD), wide),
            pltpu.VMEM((items, 2 * TILE, HD), low),
            pltpu.VMEM((2, seq, HD), low),
            pltpu.VMEM((2, seq, HD), low),
            pltpu.VMEM((2, BLK, KVH * HD), low),
            pltpu.VMEM((2, BLK, KVH * HD), low),
            pltpu.VMEM((2, 8, BLK), wide),
            pltpu.VMEM((2, 8, BLK), wide),
            pltpu.VMEM((dp, 8, BLK), wide),
            pltpu.SemaphoreType.DMA((2 * items,)),
            pltpu.SemaphoreType.DMA((2 * items,)),
            pltpu.SemaphoreType.DMA((8,)),
            pltpu.SemaphoreType.DMA((8,)),
            pltpu.SemaphoreType.DMA((1,)),
            pltpu.SemaphoreType.DMA((4,)),
            pltpu.SemaphoreType.DMA((4,)),
            pltpu.SemaphoreType.DMA((11,)),
            pltpu.SemaphoreType.DMA((6,)),
        ],
        compiler_params=pltpu.CompilerParams(
            collective_id=0, has_side_effects=True, vmem_limit_bytes=60 * 1024 * 1024
        ),
        name="attention_exchange",
    )(block_mask.transpose(1, 2, 0), queries, out_grad, keys, values)
    return pl.pallas_call(
        finish_kernel,
        out_shape=(
            shape(queries.shape, low), shape(keys.shape, low), shape(keys.shape, low),
            shape((H // 8,), wide),
        ),
        in_specs=[vmem, vmem, vmem, smem],
        out_specs=(hbm, hbm, hbm, smem),
        scratch_shapes=[pltpu.SemaphoreType.DMA((3,))],
        compiler_params=pltpu.CompilerParams(vmem_limit_bytes=62 * 1024 * 1024),
        name="write_results",
    )(*results)


def solution(mesh):
    quad = mesh.shape["ctx"] == 8
    return jax.shard_map(
        quad_body if quad else body,
        mesh=mesh,
        in_specs=(
            P("dp", "ctx", None),
            P("dp", "ctx", None),
            P("dp", "ctx", None),
            P("dp", "ctx", None),
            P(),
        ),
        out_specs=(P("dp", "ctx", None), P("dp", "ctx", None), P("dp", "ctx", None), P("ctx")),
        check_vma=False,
    )
```

profile of v0, /device:TPU:0, one launch (start us, length us, event | category | flops | bytes accessed | tf_op | source)
XLA Modules:
  0.0 59.0 jit_solution(3090477894863981183)
XLA Ops:
  0.6 55.3 %attention_exchange.1 = (bf16[1,128,4096]{2,1,0:T(8,128)(2,1)}, bf16[1,128,1024]{2,1,0:T(8,128)(2,1)}, bf16[1,128,1024]{2,1,0:T(8,128)(2,1)}, f32[8,128]{1,0:T(8,128)}) custom-call(s32[8,8,32]{2,1,0:T(8,128)} %bitcast.1, bf16[1,128,4096]{2,1,0:T(8,128)(2,1)} %q_in.1, bf16[1,128,4096]{2,1,0:T(8,128)(2,1)} %g_in.1, bf16[1,128,1024]{2,1,0:T(8,128)(2,1)} %k_in.1, ...), custom_call_target="tpu_custom_call" | custom-call | tf_op jit(solution)/shard_map/attention_exchange/pallas_call | solution.py:679
  55.9 3.0 %write_results.1 = (bf16[1,128,4096]{2,1,0:T(8,128)(2,1)}, bf16[1,128,1024]{2,1,0:T(8,128)(2,1)}, bf16[1,128,1024]{2,1,0:T(8,128)(2,1)}, f32[4]{0:T(128)}) custom-call(bf16[1,128,4096]{2,1,0:T(8,128)(2,1)} %get-tuple-element.8.dq, bf16[1,128,1024]{2,1,0:T(8,128)(2,1)} %get-tuple-element.9.dk, bf16[1,128,1024]{2,1,0:T(8,128)(2,1)} %get-tuple-element.10.dv, ...), custom_call_target="tpu_custom_call" | custom-call | tf_op jit(solution)/shard_map/write_results/pallas_call | solution.py:722
where the time goes:
time: 59.2 us; the launch traced here: 59 us
  Pallas kernels  58.3 us (98%)
  between operations  0.64 us (1%)
    pallas_call x1, Pallas kernels, quad_body(): pl.pallas_call(functools.partial(quad_kernel, dp), out_shape=(shape(queri...  55.3 us
    pallas_call x1, Pallas kernels, quad_body(): pl.pallas_call(finish_kernel, out_shape=(shape(queries.shape, low), shape...  3.03 us

commit v1 on v0

--- a/solution.py
+++ b/solution.py
@@ -470,35 +470,34 @@
                 q_tr=q.astype(jnp.float32).T.astype(jnp.bfloat16), g_tr=g_f32.astype(jnp.bfloat16),
             ))
 
-        def bias(t, c):
-            parts = []
-            for b in range(2):
-                left = mask[2 * t, 2 * c + b, head]
-                right = mask[2 * t + 1, 2 * c + b, head]
-                on = jnp.where(first_half, left, right).astype(jnp.float32)
-                parts.append(jnp.broadcast_to((1.0 - on) * NEG, (BLK, TILE)))
-            return jnp.concatenate(parts, axis=0)
-
-        for w in work:
-            w["raw"] = dot(k_all[group, w["span"], :], w["q_tr"])
+        def bias(t, block):
+            left = mask[2 * t, block, head]
+            right = mask[2 * t + 1, block, head]
+            on = jnp.where(first_half, left, right).astype(jnp.float32)
+            return (1.0 - on) * NEG
+
         for w in work:
             t, slot = w["t"], w["slot"]
             top = jnp.full((8, TILE), NEG, jnp.float32)
+            w["bias"] = [bias(t, block) for block in range(2 * t + 2)]
             for c in range(t + 1):
-                s = w["raw"][c * TILE:(c + 1) * TILE] * (scale * LOG2E) + bias(t, c)
+                at = rows(c, TILE)
+                raw = dot(k_all[group, at, :], w["q_tr"])
                 if c == t:
-                    s = jnp.where(causal, s, NEG)
-                score[slot, rows(c, TILE), :] = s
-                top = jnp.maximum(top, fold(s, jnp.max))
+                    raw = jnp.where(causal, raw, NEG)
+                score[slot, at, :] = raw
+                for b in range(2):
+                    best = fold(raw[b * BLK:(b + 1) * BLK], jnp.max) * (scale * LOG2E)
+                    top = jnp.maximum(top, best + w["bias"][2 * c + b])
             w["top"] = jnp.max(top, axis=0, keepdims=True)
-        for w in work:
-            w["pull"] = dot(v_all[group, w["span"], :], w["g_tr"])
         for w in work:
             t, slot = w["t"], w["slot"]
             total = jnp.zeros((8, TILE), jnp.float32)
-            for c in range(t + 1):
-                at = rows(c, TILE)
-                e = jnp.exp2(score[slot, at, :] - w["top"])
+            for block in range(2 * t + 2):
+                at = rows(block, BLK)
+                e = jnp.exp2(
+                    score[slot, at, :] * (scale * LOG2E) + (w["bias"][block] - w["top"])
+                )
                 score[slot, at, :] = e
                 p_low[slot, at, :] = e.astype(jnp.bfloat16)
                 total = total + fold(e, jnp.sum)
@@ -516,7 +515,7 @@
             for c in range(t + 1):
                 at = rows(c, TILE)
                 p = score[slot, at, :] * inverse
-                ds = p * (w["pull"][c * TILE:(c + 1) * TILE] - shift)
+                ds = p * (dot(v_all[group, at, :], w["g_tr"]) - shift)
                 p_low[slot, at, :] = p.astype(jnp.bfloat16)
                 ds_low[slot, at, :] = ds.astype(jnp.bfloat16)
         for w in work:
@@ -655,16 +654,26 @@
     wait_for(z_all.at[pl.ds(0, dp - 1)], z_sem.at[4])
 
 
-def finish_kernel(dq, dk, dv, z, dq_out, dk_out, dv_out, z_out, sem):
-    copies = [
-        pltpu.make_async_copy(a, b, sem.at[i])
-        for i, (a, b) in enumerate(((dq, dq_out), (dk, dk_out), (dv, dv_out)))
-    ]
-    for copy in copies:
+def finish_kernel(
+    dq, dk, dv, z, dq_out, dk_out, dv_out, z_out, dq_buf, dk_buf, dv_buf, in_sem, out_sem
+):
+    first, second = [], []
+    for src, buf, dst, parts in (
+        (dq, dq_buf, dq_out, 4), (dk, dk_buf, dk_out, 1), (dv, dv_buf, dv_out, 1)
+    ):
+        size = src.shape[1] // parts
+        for i in range(parts):
+            at, k = pl.ds(i * size, size), len(first)
+            first.append(pltpu.make_async_copy(src.at[:, at], buf.at[:, at], in_sem.at[k]))
+            second.append(pltpu.make_async_copy(buf.at[:, at], dst.at[:, at], out_sem.at[k]))
+    for copy in first:
         copy.start()
     for h in range(z_out.shape[0]):
         z_out[h] = z[h, 0]
-    for copy in copies:
+    for before, after in zip(first, second):
+        before.wait()
+        after.start()
+    for copy in second:
         copy.wait()
 
 
@@ -725,9 +734,13 @@
             shape(queries.shape, low), shape(keys.shape, low), shape(keys.shape, low),
             shape((H // 8,), wide),
         ),
-        in_specs=[vmem, vmem, vmem, smem],
+        in_specs=[hbm, hbm, hbm, smem],
         out_specs=(hbm, hbm, hbm, smem),
-        scratch_shapes=[pltpu.SemaphoreType.DMA((3,))],
+        scratch_shapes=[
+            pltpu.VMEM(queries.shape, low), pltpu.VMEM(keys.shape, low),
+            pltpu.VMEM(keys.shape, low),
+            pltpu.SemaphoreType.DMA((6,)), pltpu.SemaphoreType.DMA((6,)),
+        ],
         compiler_params=pltpu.CompilerParams(vmem_limit_bytes=62 * 1024 * 1024),
         name="write_results",
     )(*results)

time: 59.2 us -> 58.2 us (0.983)
  Pallas kernels: 58.3 us -> 57.3 us
    pallas_call x1, Pallas kernels: 55.3 us -> 53.9 us  [quad_body(): pl.pallas_call(functools.partial(quad_kernel, dp), out_shape=(shape(queri...]
where the time goes in v1:
time: 58.2 us; the launch traced here: 57.9 us
  Pallas kernels  57.3 us (98%)
  between operations  0.64 us (1%)
    pallas_call x1, Pallas kernels, quad_body(): pl.pallas_call(functools.partial(quad_kernel, dp), out_shape=(shape(queri...  53.9 us
    pallas_call x1, Pallas kernels, quad_body(): pl.pallas_call(finish_kernel, out_shape=(shape(queries.shape, low), shape...  3.43 us

profile of v1, /device:TPU:0, one launch (start us, length us, event | category | flops | bytes accessed | tf_op | source)
XLA Modules:
  0.0 57.9 jit_solution(4058122747191600713)
XLA Ops:
  0.6 53.9 %attention_exchange.1 = (bf16[1,128,4096]{2,1,0:T(8,128)(2,1)}, bf16[1,128,1024]{2,1,0:T(8,128)(2,1)}, bf16[1,128,1024]{2,1,0:T(8,128)(2,1)}, f32[8,128]{1,0:T(8,128)}) custom-call(s32[8,8,32]{2,1,0:T(8,128)} %bitcast.1, bf16[1,128,4096]{2,1,0:T(8,128)(2,1)} %q_in.1, bf16[1,128,4096]{2,1,0:T(8,128)(2,1)} %g_in.1, bf16[1,128,1024]{2,1,0:T(8,128)(2,1)} %k_in.1, ...), custom_call_target="tpu_custom_call" | custom-call | tf_op jit(solution)/shard_map/attention_exchange/pallas_call | solution.py:688
  54.5 3.4 %write_results.1 = (bf16[1,128,4096]{2,1,0:T(8,128)(2,1)}, bf16[1,128,1024]{2,1,0:T(8,128)(2,1)}, bf16[1,128,1024]{2,1,0:T(8,128)(2,1)}, f32[4]{0:T(128)}) custom-call(bf16[1,128,4096]{2,1,0:T(8,128)(2,1)} %get-tuple-element.8.dq, bf16[1,128,1024]{2,1,0:T(8,128)(2,1)} %get-tuple-element.9.dk, bf16[1,128,1024]{2,1,0:T(8,128)(2,1)} %get-tuple-element.10.dv, ...), custom_call_target="tpu_custom_call" | custom-call | tf_op jit(solution)/shard_map/write_results/pallas_call | solution.py:731

commit v2 on v1

--- a/solution.py
+++ b/solution.py
@@ -429,16 +429,10 @@
 
         lax.fori_loop(0, 4, one, 0)
 
-    def send_pair(m, c):
-        send_q(0, m)
-        send_q(1, m)
-        return c
-
     send_kv(0)
     send_q(0, 0)
     send_kv(1)
     send_q(1, 0)
-    lax.fori_loop(1, per, send_pair, 0)
 
     z_own[...] = jnp.zeros_like(z_own)
     dk_acc[...] = jnp.zeros_like(dk_acc)
@@ -576,8 +570,12 @@
             lax.fori_loop(0, high + 1, give, 0)
 
     def one_step(m, carry):
-        one_item(0, m)
-        one_item(1, m)
+        for group in range(2):
+            @pl.when(m + 1 < per)
+            def _(group=group):
+                send_q(group, m + 1)
+
+            one_item(group, m)
         return carry
 
     lax.fori_loop(0, per, one_step, 0)
@@ -654,26 +652,16 @@
     wait_for(z_all.at[pl.ds(0, dp - 1)], z_sem.at[4])
 
 
-def finish_kernel(
-    dq, dk, dv, z, dq_out, dk_out, dv_out, z_out, dq_buf, dk_buf, dv_buf, in_sem, out_sem
-):
-    first, second = [], []
-    for src, buf, dst, parts in (
-        (dq, dq_buf, dq_out, 4), (dk, dk_buf, dk_out, 1), (dv, dv_buf, dv_out, 1)
-    ):
-        size = src.shape[1] // parts
-        for i in range(parts):
-            at, k = pl.ds(i * size, size), len(first)
-            first.append(pltpu.make_async_copy(src.at[:, at], buf.at[:, at], in_sem.at[k]))
-            second.append(pltpu.make_async_copy(buf.at[:, at], dst.at[:, at], out_sem.at[k]))
-    for copy in first:
+def finish_kernel(dq, dk, dv, z, dq_out, dk_out, dv_out, z_out, sem):
+    copies = [
+        pltpu.make_async_copy(a, b, sem.at[i])
+        for i, (a, b) in enumerate(((dq, dq_out), (dk, dk_out), (dv, dv_out)))
+    ]
+    for copy in copies:
         copy.start()
     for h in range(z_out.shape[0]):
         z_out[h] = z[h, 0]
-    for before, after in zip(first, second):
-        before.wait()
-        after.start()
-    for copy in second:
+    for copy in copies:
         copy.wait()
 
 
@@ -734,13 +722,9 @@
             shape(queries.shape, low), shape(keys.shape, low), shape(keys.shape, low),
             shape((H // 8,), wide),
         ),
-        in_specs=[hbm, hbm, hbm, smem],
+        in_specs=[vmem, vmem, vmem, smem],
         out_specs=(hbm, hbm, hbm, smem),
-        scratch_shapes=[
-            pltpu.VMEM(queries.shape, low), pltpu.VMEM(keys.shape, low),
-            pltpu.VMEM(keys.shape, low),
-            pltpu.SemaphoreType.DMA((6,)), pltpu.SemaphoreType.DMA((6,)),
-        ],
+        scratch_shapes=[pltpu.SemaphoreType.DMA((3,))],
         compiler_params=pltpu.CompilerParams(vmem_limit_bytes=62 * 1024 * 1024),
         name="write_results",
     )(*results)

time: 58.2 us -> 60.7 us (1.043)
  Pallas kernels: 57.3 us -> 59.9 us
    pallas_call x1, Pallas kernels: 53.9 us -> 56.8 us  [quad_body(): pl.pallas_call(functools.partial(quad_kernel, dp), out_shape=(shape(queri...]
where the time goes in v2:
time: 60.7 us; the launch traced here: 60.5 us
  Pallas kernels  59.9 us (99%)
  between operations  0.64 us (1%)
    pallas_call x1, Pallas kernels, quad_body(): pl.pallas_call(functools.partial(quad_kernel, dp), out_shape=(shape(queri...  56.8 us
    pallas_call x1, Pallas kernels, quad_body(): pl.pallas_call(finish_kernel, out_shape=(shape(queries.shape, low), shape...  3.03 us

profile of v2, /device:TPU:0, one launch (start us, length us, event | category | flops | bytes accessed | tf_op | source)
XLA Modules:
  0.0 60.5 jit_solution(17196239591244105378)
XLA Ops:
  0.6 56.8 %attention_exchange.1 = (bf16[1,128,4096]{2,1,0:T(8,128)(2,1)}, bf16[1,128,1024]{2,1,0:T(8,128)(2,1)}, bf16[1,128,1024]{2,1,0:T(8,128)(2,1)}, f32[8,128]{1,0:T(8,128)}) custom-call(s32[8,8,32]{2,1,0:T(8,128)} %bitcast.1, bf16[1,128,4096]{2,1,0:T(8,128)(2,1)} %q_in.1, bf16[1,128,4096]{2,1,0:T(8,128)(2,1)} %g_in.1, bf16[1,128,1024]{2,1,0:T(8,128)(2,1)} %k_in.1, ...), custom_call_target="tpu_custom_call" | custom-call | tf_op jit(solution)/shard_map/attention_exchange/pallas_call | solution.py:676
  57.5 3.0 %write_results.1 = (bf16[1,128,4096]{2,1,0:T(8,128)(2,1)}, bf16[1,128,1024]{2,1,0:T(8,128)(2,1)}, bf16[1,128,1024]{2,1,0:T(8,128)(2,1)}, f32[4]{0:T(128)}) custom-call(bf16[1,128,4096]{2,1,0:T(8,128)(2,1)} %get-tuple-element.8.dq, bf16[1,128,1024]{2,1,0:T(8,128)(2,1)} %get-tuple-element.9.dk, bf16[1,128,1024]{2,1,0:T(8,128)(2,1)} %get-tuple-element.10.dv, ...), custom_call_target="tpu_custom_call" | custom-call | tf_op jit(solution)/shard_map/write_results/pallas_call | solution.py:719

commit v3 on v2

--- a/solution.py
+++ b/solution.py
@@ -411,8 +411,9 @@
 
         lax.fori_loop(0, n, one, 0)
 
-    def send_q(group, m):
-        item = 2 * m + group
+    pieces = (pl.ds(0, HD), pl.ds(HD, (per - 1) * HD))
+
+    def send_q(group, piece):
         slot = x if group == 0 else y
         place = rows(2 * slot + core, tok)
 
@@ -421,10 +422,11 @@
             to = 2 * far + lax.rem(core + j, 2) + (4 * y if group == 0 else 0)
             if group == 1:
                 to = 4 * far + 2 * x + lax.rem(core + j, 2)
-            col = lanes(kv_head(group, to) * per + m)
-            at = item * 2 + slot
-            move(q_in.at[0, :, col], q_all.at[item, place], send_sem.at[4], q_sem.at[at], to)
-            move(g_in.at[0, :, col], g_all.at[item, place], send_sem.at[5], g_sem.at[at], to)
+            first = pl.multiple_of((kv_head(group, to) * per + piece) * HD, HD)
+            col, put = pl.ds(first, pieces[piece].size), pieces[piece]
+            at = (group * 2 + slot) * 2 + piece
+            move(q_in.at[0, :, col], q_all.at[group, place, put], send_sem.at[4], q_sem.at[at], to)
+            move(g_in.at[0, :, col], g_all.at[group, place, put], send_sem.at[5], g_sem.at[at], to)
             return c
 
         lax.fori_loop(0, 4, one, 0)
@@ -433,6 +435,8 @@
     send_q(0, 0)
     send_kv(1)
     send_q(1, 0)
+    send_q(0, 1)
+    send_q(1, 1)
 
     z_own[...] = jnp.zeros_like(z_own)
     dk_acc[...] = jnp.zeros_like(dk_acc)
@@ -456,8 +460,8 @@
     def tile_pair(pair, group, head, item):
         work = []
         for slot, t in ((1, pair[1]), (0, pair[0])):
-            q = q_all[item, rows(slot, TILE), :]
-            g = g_all[item, rows(slot, TILE), :]
+            q = q_all[group, rows(slot, TILE), lanes(item // 2)]
+            g = g_all[group, rows(slot, TILE), lanes(item // 2)]
             g_f32 = g.astype(jnp.float32).T
             work.append(dict(
                 slot=slot, t=t, span=pl.ds(0, (t + 1) * TILE), q=q, g=g, g_f32=g_f32,
@@ -532,9 +536,14 @@
         def _():
             prepare(group, high)
 
-        for slot in range(2):
-            wait_for(q_all.at[item, rows(slot, TILE)], q_sem.at[item * 2 + slot])
-            wait_for(g_all.at[item, rows(slot, TILE)], g_sem.at[item * 2 + slot])
+        for piece in range(2):
+            @pl.when(m == piece)
+            def _(piece=piece):
+                for slot in range(2):
+                    place, at = rows(slot, TILE), (group * 2 + slot) * 2 + piece
+                    wait_for(q_all.at[group, place, pieces[piece]], q_sem.at[at])
+                    wait_for(g_all.at[group, place, pieces[piece]], g_sem.at[at])
+
         for choice, pair in enumerate(((0, 1), (2, 3)) if group == 0 else ((0, 2), (1, 3))):
             @pl.when(half == choice)
             def _(pair=pair):
@@ -570,12 +579,8 @@
             lax.fori_loop(0, high + 1, give, 0)
 
     def one_step(m, carry):
-        for group in range(2):
-            @pl.when(m + 1 < per)
-            def _(group=group):
-                send_q(group, m + 1)
-
-            one_item(group, m)
+        one_item(0, m)
+        one_item(1, m)
         return carry
 
     lax.fori_loop(0, per, one_step, 0)
@@ -682,8 +687,8 @@
         in_specs=[smem] + [hbm] * 4,
         out_specs=(hbm, vmem, vmem, vmem),
         scratch_shapes=[
-            pltpu.VMEM((items, 2 * TILE, HD), low),
-            pltpu.VMEM((items, 2 * TILE, HD), low),
+            pltpu.VMEM((2, 2 * TILE, items // 2 * HD), low),
+            pltpu.VMEM((2, 2 * TILE, items // 2 * HD), low),
             pltpu.VMEM((2, seq, HD), low),
             pltpu.VMEM((2, seq, HD), low),
             pltpu.VMEM((2, HD, seq), low),
@@ -701,8 +706,8 @@
             pltpu.VMEM((2, 8, BLK), wide),
             pltpu.VMEM((2, 8, BLK), wide),
             pltpu.VMEM((dp, 8, BLK), wide),
-            pltpu.SemaphoreType.DMA((2 * items,)),
-            pltpu.SemaphoreType.DMA((2 * items,)),
+            pltpu.SemaphoreType.DMA((items,)),
+            pltpu.SemaphoreType.DMA((items,)),
             pltpu.SemaphoreType.DMA((8,)),
             pltpu.SemaphoreType.DMA((8,)),
             pltpu.SemaphoreType.DMA((1,)),

time: 60.7 us -> 62.6 us (1.031)
  Pallas kernels: 59.9 us -> 61.7 us
    pallas_call x1, Pallas kernels: 56.8 us -> 58.7 us  [quad_body(): pl.pallas_call(functools.partial(quad_kernel, dp), out_shape=(shape(queri...]
where the time goes in v3:
time: 62.6 us; the launch traced here: 62.4 us
  Pallas kernels  61.7 us (99%)
  between operations  0.64 us (1%)
    pallas_call x1, Pallas kernels, quad_body(): pl.pallas_call(functools.partial(quad_kernel, dp), out_shape=(shape(queri...  58.7 us
    pallas_call x1, Pallas kernels, quad_body(): pl.pallas_call(finish_kernel, out_shape=(shape(queries.shape, low), shape...  3.03 us

profile of v3, /device:TPU:0, one launch (start us, length us, event | category | flops | bytes accessed | tf_op | source)
XLA Modules:
  0.0 62.4 jit_solution(3912329320372606090)
XLA Ops:
  0.6 58.7 %attention_exchange.1 = (bf16[1,128,4096]{2,1,0:T(8,128)(2,1)}, bf16[1,128,1024]{2,1,0:T(8,128)(2,1)}, bf16[1,128,1024]{2,1,0:T(8,128)(2,1)}, f32[8,128]{1,0:T(8,128)}) custom-call(s32[8,8,32]{2,1,0:T(8,128)} %bitcast.1, bf16[1,128,4096]{2,1,0:T(8,128)(2,1)} %q_in.1, bf16[1,128,4096]{2,1,0:T(8,128)(2,1)} %g_in.1, bf16[1,128,1024]{2,1,0:T(8,128)(2,1)} %k_in.1, ...), custom_call_target="tpu_custom_call" | custom-call | tf_op jit(solution)/shard_map/attention_exchange/pallas_call | solution.py:681
  59.3 3.0 %write_results.1 = (bf16[1,128,4096]{2,1,0:T(8,128)(2,1)}, bf16[1,128,1024]{2,1,0:T(8,128)(2,1)}, bf16[1,128,1024]{2,1,0:T(8,128)(2,1)}, f32[4]{0:T(128)}) custom-call(bf16[1,128,4096]{2,1,0:T(8,128)(2,1)} %get-tuple-element.8.dq, bf16[1,128,1024]{2,1,0:T(8,128)(2,1)} %get-tuple-element.9.dk, bf16[1,128,1024]{2,1,0:T(8,128)(2,1)} %get-tuple-element.10.dv, ...), custom_call_target="tpu_custom_call" | custom-call | tf_op jit(solution)/shard_map/write_results/pallas_call | solution.py:724
